TPU v7x, 256 devices: a whole 4x4x8 slice. The times are simulated.
256 devices in a mesh: frame: 32 (over z_hi, x, core), head: 4 (over y), batch: 2 (over z_lo).
Axes of the slice: x: 4, y: 4, z: 8 (z_hi: 4, z_lo: 2; z = z_hi * 2 + z_lo), core: 2. Of those that a mesh axis runs over, the one named last changes fastest.
Arguments:
- new_qkv: bfloat16 [4096, 3, 3072], P(('batch', 'frame', 'head')), parts along dimension 0, may hold values from -16 to 16
- new_pos: int32 [6, 2048], P('batch', 'frame'), parts along dimension 0, may hold values from 0 to 31, as said below
- cache_keys: bfloat16 [2048, 3072], P(('batch', 'frame'), 'head'), parts along dimension 0, may hold values from -48 to 48
- cache_values: bfloat16 [2048, 3072], P(('batch', 'frame'), 'head'), parts along dimension 0, may hold values from -6 to 6
- cache_pos: int32 [6, 1024], P('batch', 'frame'), parts along dimension 0, may hold values from 0 to 31, as said below
- cache_shot: int32 [2048], P(('batch', 'frame')), parts along dimension 0, may hold values from 0 to 2, as said below
- out_weight: bfloat16 [3072, 3072], P('head'), may hold values from -0.4375 to 0.4375
Outputs:
- shot_out: bfloat16 [4096, 3072], P(('batch', 'frame', 'head')), parts along dimension 0
There are 2 independent parts, one for each index of `batch`. A program takes and returns all parts, laid end to end along the dimension named above; an argument that names none is the same for every part. Nothing has to cross between parts.
Inputs may be any that keep to these rules, and one draw needn't show every extreme that they name: `new_pos`: component 0 lies below 8, components 1 and 2 below 32. `cache_pos`: component 0 lies below 8, components 1 and 2 below 32. `cache_shot`: never falls along the cache; every one of the 3 shots is present.
All inputs are finite; a program needn't handle non-finite values.
Results may differ from a plain program's by a relative error of at most 0.015.
The roundings to bfloat16 on the way count: a program that leaves them out, or rounds other values in their place, can miss the bound.
Values may be sent and summed in bfloat16 or wider, within the bound.
A program may use at most 128 MiB of HBM per device.

v0:
```python
import math

import jax
import jax.numpy as jnp
from jax import lax
from jax.sharding import PartitionSpec as P

HEAD_DIM = 128
SHOTS = 3
SHOT_FRAMES = 8


THETA = 10000.0


def rope_angles(temporal, row_pos, column_pos, feature_width, head_dim):
    lanes = jnp.arange(feature_width, dtype=jnp.int32) % head_dim
    pairs = lanes // 2
    time_pairs = head_dim // 16
    row_pairs = (head_dim // 2 - time_pairs) // 2
    rest_pairs = head_dim // 2 - time_pairs - row_pairs
    in_time = pairs < time_pairs
    in_row = (pairs >= time_pairs) & (pairs < time_pairs + row_pairs)
    pair_float = pairs.astype(jnp.float32)
    exponent = jnp.where(
        in_time,
        pair_float / time_pairs,
        jnp.where(
            in_row,
            (pair_float - time_pairs) / row_pairs,
            (pair_float - time_pairs - row_pairs) / rest_pairs,
        ),
    )
    frequency = jnp.power(jnp.float32(THETA), -exponent)
    position = jnp.where(
        in_time[None, :],
        temporal[:, None],
        jnp.where(in_row[None, :], row_pos[:, None], column_pos[:, None]),
    ).astype(jnp.float32)
    return position * frequency[None, :]


def rotate(values_in, angles):
    feature_width = values_in.shape[-1]
    even = jnp.arange(feature_width, dtype=jnp.int32) % 2 == 0
    partner = jnp.where(even, -jnp.roll(values_in, -1, axis=-1), jnp.roll(values_in, 1, axis=-1))
    return values_in * jnp.cos(angles) + partner * jnp.sin(angles)


def on_device(new_qkv, new_pos, cache_keys, cache_values, cache_pos, cache_shot, out_weight):
    feature_width = cache_keys.shape[1]
    head_count = feature_width // HEAD_DIM
    score_scale = 1.0 / math.sqrt(HEAD_DIM)
    cache_angles = rope_angles(
        cache_shot * SHOT_FRAMES + cache_pos[0], cache_pos[1], cache_pos[2], feature_width, HEAD_DIM
    )
    cached_keys = rotate(cache_keys.astype(jnp.float32), cache_angles).astype(jnp.bfloat16)
    mixed = lax.all_to_all(new_qkv, "head", split_axis=2, concat_axis=0, tiled=True)
    new_angles = rope_angles(
        SHOTS * SHOT_FRAMES + new_pos[0], new_pos[1], new_pos[2], feature_width, HEAD_DIM
    )
    queries = rotate(mixed[:, 0].astype(jnp.float32), new_angles).astype(jnp.bfloat16)
    new_keys = rotate(mixed[:, 1].astype(jnp.float32), new_angles).astype(jnp.bfloat16)
    new_values = mixed[:, 2]
    row_count = queries.shape[0]
    joined_keys = jnp.concatenate([cached_keys, new_keys], axis=0)
    joined_values = jnp.concatenate([cache_values, new_values], axis=0)
    peaks = jnp.full((head_count, row_count), -1e30, jnp.float32)
    totals = jnp.zeros((head_count, row_count), jnp.float32)
    accums = jnp.zeros((row_count, feature_width), jnp.float32)
    key_rows = lax.all_gather(joined_keys, "frame", axis=0, tiled=True)
    value_rows = lax.all_gather(joined_values, "frame", axis=0, tiled=True)
    peak_list = []
    total_list = []
    accum_list = []
    for head in range(head_count):
        lanes = slice(head * HEAD_DIM, (head + 1) * HEAD_DIM)
        scores = (
            lax.dot_general(
                queries[:, lanes],
                key_rows[:, lanes],
                (((1,), (1,)), ((), ())),
                preferred_element_type=jnp.float32,
            )
            * score_scale
        )
        peak = jnp.maximum(peaks[head], jnp.max(scores, axis=1))
        weights = jnp.exp(scores - peak[:, None])
        shrink = jnp.exp(peaks[head] - peak)
        total_list.append(totals[head] * shrink + jnp.sum(weights, axis=1))
        accum_list.append(
            accums[:, lanes] * shrink[:, None]
            + jnp.dot(
                weights.astype(jnp.bfloat16),
                value_rows[:, lanes],
                preferred_element_type=jnp.float32,
            )
        )
        peak_list.append(peak)
    attended = (
        jnp.concatenate(accum_list, axis=1) / jnp.repeat(jnp.stack(total_list).T, HEAD_DIM, axis=1)
    ).astype(jnp.bfloat16)
    return lax.psum_scatter(
        jnp.dot(attended, out_weight, preferred_element_type=jnp.float32).astype(jnp.bfloat16),
        "head",
        scatter_dimension=0,
        tiled=True,
    )


def solution(mesh):
    placed = (
        P(("batch", "frame", "head"), None, None),
        P("batch", "frame"),
        P(("batch", "frame"), "head"),
        P(("batch", "frame"), "head"),
        P("batch", "frame"),
        P(("batch", "frame")),
        P("head", None),
    )
    return jax.shard_map(
        on_device,
        mesh=mesh,
        in_specs=placed,
        out_specs=P(("batch", "frame", "head"), None),
        check_vma=False,
    )
```

profile of v0, /device:TPU:1, one launch (start us, length us, event | category | flops | bytes accessed | tf_op | source)
XLA Modules:
  0.0 196.6 jit_solution(4927370221826058485)
XLA Ops:
  6.5 4.2 %copy.13 = bf16[16,3,3072]{0,1,2:T(4,128)(2,1)S(1)} copy(bf16[16,3,3072]{2,0,1:T(8,128)(2,1)} %param.7) | data formatting | bytes 589824 | tf_op args[0]
  10.8 3.4 %reshape.292 = bf16[4,2,18432]{2,1,0:T(2,128)(2,1)} reshape(bf16[3072,3,16]{2,1,0:T(4,128)(2,1)S(1)} %bitcast.56) | data formatting | bytes 589824
  14.1 5.0 %all-to-all-start = ((bf16[4,2,18432]{2,1,0:T(2,128)(2,1)}), bf16[4,2,18432]{2,1,0:T(2,128)(2,1)S(1)}, u32[]{:S(2)}, u32[]{:S(2)}) async-start(bf16[4,2,18432]{2,1,0:T(2,128)(2,1)} %reshape.292), calls=%async_computation | async-start | bytes 589824 | tf_op jit(solution)/shard_map/all_to_all | solution.py:58
  19.2 0.1 fusion.81
  19.3 0.1 fusion.80
  19.4 0.5 fusion.59
  19.9 1.3 add_bitcast_fusion.6
  21.2 3.7 %all-to-all-done = bf16[4,2,18432]{2,1,0:T(2,128)(2,1)S(1)} async-done(((bf16[4,2,18432]{2,1,0:T(2,128)(2,1)}), bf16[4,2,18432]{2,1,0:T(2,128)(2,1)S(1)}, u32[]{:S(2)}, u32[]{:S(2)}) %all-to-all-start) | async-done | bytes 294944 | tf_op jit(solution)/shard_map/all_to_all | solution.py:58
  24.8 3.0 %reshape.293 = bf16[3072,3,16]{2,1,0:T(4,128)(2,1)S(1)} reshape(bf16[4,2,18432]{2,1,0:T(2,128)(2,1)S(1)} %all-to-all-done) | data formatting | bytes 589824
  27.9 0.0 copy-start.4
  27.9 1.5 copy.15
  29.5 0.2 fusion.77
  29.6 0.1 fusion.76
  29.7 0.0 copy-done.4
  29.8 1.6 fusion.46
  31.3 0.7 pad_maximum_fusion
  32.0 0.0 all-gather.3.cloned.1.call-update
  32.0 0.0 all-gather.5.cloned.1.call-start
  32.1 1.5 pad_maximum_fusion.1
  33.5 0.0 all-gather.5.cloned.1.call-update
  33.6 0.0 reduce-scatter.2.cloned.1.call-start
  33.6 64.2 %all-gather.3.cloned.1.call-done = bf16[3072,768]{1,0:T(8,128)(2,1)} async-done(((bf16[96,768]{1,0:T(8,128)(2,1)}), bf16[3072,768]{1,0:T(8,128)(2,1)}) %all-gather.3.cloned.1.call-update) | async-done | bytes 4718608 | tf_op jit(solution)/shard_map/all_gather | solution.py:71
  97.8 1.7 fusion.87
  99.4 0.3 fusion.28
  99.7 1.7 fusion.86
  101.4 0.3 fusion.26
  101.7 1.7 fusion.85
  103.4 0.3 fusion.24
  103.7 1.7 fusion.84
  105.3 0.3 fusion.22
  105.6 1.7 fusion.83
  107.3 0.9 copy-done
  108.2 0.3 fusion.20
  108.5 1.7 fusion.82
  110.1 0.9 copy-done.1
  111.0 0.3 fusion.18
  111.4 0.1 copy.16
  111.5 49.4 %all-gather.5.cloned.1.call-done = bf16[3072,768]{1,0:T(8,128)(2,1)} async-done(((bf16[96,768]{1,0:T(8,128)(2,1)}), bf16[3072,768]{1,0:T(8,128)(2,1)}) %all-gather.5.cloned.1.call-update) | async-done | bytes 4718608 | tf_op jit(solution)/shard_map/all_gather | solution.py:72
  160.9 1.8 fusion.5
  162.7 1.7 fusion.4
  164.5 1.5 fusion.3
  166.0 0.3 fusion.2
  166.3 0.3 fusion.1
  166.6 0.3 fusion
  167.0 0.1 broadcast_in_dim.138
  167.1 4.0 %convolution_convert_fusion = bf16[64,3072]{1,0:T(8,128)(2,1)} fusion(bf16[768,3072]{1,0:T(8,128)(2,1)} %param.13, f32[64,768]{1,0:T(8,128)S(1)} %fusion, f32[8,8,6,128]{3,2,1,0:T(8,128)S(1)} %bitcast.59), kind=kOutput, calls=%fused_computation.6 | convolution fusion | flops 302284800 | bytes 5505024 | tf_op jit(solution)/shard_map/dot_general | solution.py:104
  171.1 0.0 reduce-scatter.2.cloned.1.call-update
  171.2 19.0 %reduce-scatter.2.cloned.1.call-done = bf16[16,3072]{1,0:T(8,128)(2,1)} async-done(((bf16[64,3072]{1,0:T(8,128)(2,1)}), bf16[16,3072]{1,0:T(8,128)(2,1)}) %reduce-scatter.2.cloned.1.call-update) | async-done | bytes 98320 | tf_op jit(solution)/shard_map/reduce_scatter | solution.py:103
  (34 shorter events, 0.2 us)
Async XLA Ops:
  6.5 12.7 %copy-start.3 = (bf16[32,768]{1,0:T(8,128)(2,1)S(1)}, bf16[32,768]{1,0:T(8,128)(2,1)}, u32[]{:S(2)}) copy-start(bf16[32,768]{1,0:T(8,128)(2,1)} %param.9) | copy-start | bytes 147460
  6.5 12.8 %copy-start.7 = (s32[3,32]{1,0:T(4,128)S(1)}, s32[3,32]{1,0:T(4,128)}, u32[]{:S(2)}) copy-start(s32[3,32]{1,0:T(4,128)} %param.11) | copy-start | bytes 1156
  6.5 12.8 %copy-start.8 = (s32[32]{0:T(128)S(1)}, s32[32]{0:T(128)}, u32[]{:S(2)}) copy-start(s32[32]{0:T(128)} %param.12) | copy-start | bytes 388
  14.1 10.7 %all-to-all-start = ((bf16[4,2,18432]{2,1,0:T(2,128)(2,1)}), bf16[4,2,18432]{2,1,0:T(2,128)(2,1)S(1)}, u32[]{:S(2)}, u32[]{:S(2)}) async-start(bf16[4,2,18432]{2,1,0:T(2,128)(2,1)} %reshape.292), calls=%async_computation | async-start | bytes 589824 | tf_op jit(solution)/shard_map/all_to_all | solution.py:58
  19.1 78.6 %all-gather.3.cloned.1.call-start = ((), (), s32[]{:S(2)}) async-start(), calls=%async_computation.2 | async-start | bytes 4866048 | tf_op jit(solution)/shard_map/all_gather | solution.py:71
  27.9 1.9 copy-start.4
  27.9 1.9 copy-start.5
  27.9 1.9 copy-start.6
  32.0 128.9 %all-gather.5.cloned.1.call-start = ((), (), s32[]{:S(2)}) async-start(), calls=%async_computation.3 | async-start | bytes 4866048 | tf_op jit(solution)/shard_map/all_gather | solution.py:72
  33.6 156.5 %reduce-scatter.2.cloned.1.call-start = ((), (), s32[]{:S(2)}) async-start(), calls=%async_computation.4 | async-start | bytes 491520 | tf_op jit(solution)/shard_map/reduce_scatter | solution.py:103
  107.3 0.9 copy-start
  110.1 0.9 copy-start.1
  160.9 5.1 %copy-start.2 = (bf16[3072,768]{1,0:T(8,128)(2,1)S(1)}, bf16[3072,768]{1,0:T(8,128)(2,1)}, u32[]{:S(2)}) copy-start(bf16[3072,768]{1,0:T(8,128)(2,1)} %all-gather.5.cloned.1.call-done) | copy-start | bytes 14155780
Sparse Core Ops, SparseCore 0:
  32.1 65.5 all-gather.2
  100.3 60.5 all-gather.4
  171.3 18.7 reduce-scatter.1
where the time goes:
time: 198 us; the launch traced here: 197 us
  waiting for transfers between devices  136 us (69%)
  matrix products  20 us (10%)
  local copies, waits for them, and re-layouts  14.6 us (7%)
  between operations  13.4 us (7%)
  other arithmetic  7.38 us (4%)
  starting transfers between devices  5.1 us (3%)
    all_gather x1, waiting for transfers between devices, on_device(): key_rows = lax.all_gather(joined_keys, 'frame', axis=0, tiled=True)  64.2 us
    all_gather x1, waiting for transfers between devices, on_device(): value_rows = lax.all_gather(joined_values, 'frame', axis=0, tiled=True)  49.4 us
    reduce_scatter x1, waiting for transfers between devices, on_device(): lax.psum_scatter(jnp.dot(attended, out_weight, preferred_element_type=jnp...  19 us
    unnamed x21, local copies, waits for them, and re-layouts  12.4 us
    dot_general x6, matrix products, on_device(): lax.dot_general(queries[:, lanes], key_rows[:, lanes], (((1,), (1,)), (()...  9.93 us
    dot_general x6, matrix products, on_device(): jnp.dot(weights.astype(jnp.bfloat16), value_rows[:, lanes], preferred_ele...  6.04 us
    all_to_all x1, starting transfers between devices, on_device(): lax.all_to_all(new_qkv, 'head', split_axis=2, concat_axis=0, tiled=True)  5.01 us
    dot_general x1, matrix products, on_device(): jnp.dot(attended, out_weight, preferred_element_type=jnp.float32)  4.02 us
  transfers between devices with their start and end apart: 4, of which 4 were waited for; matrix products, arithmetic and copies ran while one was open for 8% of the time, Pallas kernels for 0%

commit v1 on v0

v1 whole, which is shorter than its diff:
```python
import functools
import math

import jax
import jax.numpy as jnp
from jax import lax
from jax.experimental import pallas as pl
from jax.experimental.pallas import tpu as pltpu
from jax.sharding import PartitionSpec as P

HEAD_DIM = 128
SHOTS = 3
SHOT_FRAMES = 8
THETA = 10000.0
RING = 4
CORES = 2
NEW_ROWS = 16
CACHE_ROWS = 32
HEADS_CORE = 3
CHIP_NEW = RING * CORES * NEW_ROWS
CHIP_CACHE = CORES * CACHE_ROWS
ALL_CACHE = RING * CHIP_CACHE
KEYS = RING * (CHIP_NEW + CHIP_CACHE)
QUERIES = RING * CHIP_NEW
OWN = RING * NEW_ROWS
D = 3072
GROUP = D // RING
CHUNKS = 4
CHUNK = D // CHUNKS
SCALE2 = math.log2(math.e) / math.sqrt(HEAD_DIM)
MESH = pl.DeviceIdType.MESH


def frequencies():
    lanes = lax.broadcasted_iota(jnp.int32, (3, HEAD_DIM), 1)
    part = lax.broadcasted_iota(jnp.int32, (3, HEAD_DIM), 0)
    pairs = lanes // 2
    time_pairs = HEAD_DIM // 16
    row_pairs = (HEAD_DIM // 2 - time_pairs) // 2
    rest_pairs = HEAD_DIM // 2 - time_pairs - row_pairs
    of_part = jnp.where(pairs < time_pairs, 0, jnp.where(pairs < time_pairs + row_pairs, 1, 2))
    pair_float = pairs.astype(jnp.float32)
    exponent = jnp.where(
        of_part == 0,
        pair_float / time_pairs,
        jnp.where(
            of_part == 1,
            (pair_float - time_pairs) / row_pairs,
            (pair_float - time_pairs - row_pairs) / rest_pairs,
        ),
    )
    return jnp.where(of_part == part, jnp.exp(exponent * -math.log(THETA)), 0.0)


def turned(block, cos, sin, even):
    x = block.astype(jnp.float32)
    partner = jnp.where(even, pltpu.roll(x, HEAD_DIM - 1, 1), pltpu.roll(x, 1, 1))
    return (x * cos + partner * sin).astype(jnp.bfloat16)


def kernel(
    qkv_hbm,
    npos_hbm,
    ck_hbm,
    cv_hbm,
    cpos_hbm,
    shot_hbm,
    w_hbm,
    out_ref,
    qkv,
    npos,
    ck,
    cv,
    cpos,
    shot,
    w,
    angles,
    stage,
    cstage,
    kv,
    q,
    o,
    lse,
    lse_t,
    ored,
    lred,
    weights,
    part,
    recv,
    in_sem,
    a_send,
    a_recv,
    c_send,
    c_recv,
    x_send,
    x_recv,
    z_send,
    z_recv,
    o_send,
    o_recv,
    l_send,
    l_recv,
    y_send,
    y_recv,
):
    frame = lax.axis_index("frame")
    y = lax.axis_index("head")
    batch = lax.axis_index("batch")
    core = lax.rem(frame, CORES)
    x = lax.rem(frame // CORES, RING)
    z = frame // (CORES * RING)

    def device(dx, dy, dz, dc):
        to = (lax.rem(z + dz, RING) * RING + lax.rem(x + dx, RING)) * CORES + lax.rem(core + dc, CORES)
        return (to, lax.rem(y + dy, RING), batch)

    barrier = pltpu.get_barrier_semaphore()
    greeted = [(0, 0, 0, 1)]
    for d in (2, 1, 3):
        for dc in (0, 1):
            greeted += [(0, 0, d, dc), (d, 0, 0, dc), (0, d, 0, dc)]
    for g in greeted:
        pl.semaphore_signal(barrier, inc=1, device_id=device(*g), device_id_type=MESH)

    loads = [
        pltpu.make_async_copy(a, b, in_sem.at[i])
        for i, (a, b) in enumerate(
            [(npos_hbm, npos), (cpos_hbm, cpos), (shot_hbm, shot), (qkv_hbm, qkv), (ck_hbm, ck), (cv_hbm, cv), (w_hbm, w)]
        )
    ]
    for load in loads:
        load.start()

    lane = lax.broadcasted_iota(jnp.int32, (1, HEAD_DIM), 1)
    even = lax.rem(lane, 2) == 0
    freq = frequencies()
    for load in loads[:3]:
        load.wait()
    first = lax.broadcasted_iota(jnp.int32, (3, 1), 0) == 0

    def angles_of(pos):
        return lax.dot_general(
            pos.astype(jnp.float32),
            freq,
            (((0,), (0,)), ((), ())),
            precision=lax.Precision.HIGHEST,
            preferred_element_type=jnp.float32,
        )

    angles[0 : RING * NEW_ROWS, :] = angles_of(npos[...] + jnp.where(first, SHOTS * SHOT_FRAMES, 0))
    angle = angles[pl.ds(pl.multiple_of(y * NEW_ROWS, NEW_ROWS), NEW_ROWS), :]
    cos = jnp.cos(angle)
    sin = jnp.where(even, -jnp.sin(angle), jnp.sin(angle))

    for load in loads[3:6]:
        load.wait()

    def rotate_new(i, carry):
        for j in range(HEADS_CORE):
            head = i * HEADS_CORE + j
            lanes = pl.ds(pl.multiple_of(head * HEAD_DIM, HEAD_DIM), HEAD_DIM)
            stage[head, 0] = turned(qkv[0, :, lanes], cos, sin, even)
            stage[head, 1] = turned(qkv[1, :, lanes], cos, sin, even)
            stage[head, 2] = qkv[2, :, lanes]
        return carry

    lax.fori_loop(0, D // (HEAD_DIM * HEADS_CORE), rotate_new, 0)
    pl.semaphore_wait(barrier, len(greeted))

    here = pl.multiple_of(core * OWN + y * NEW_ROWS, NEW_ROWS)
    q_rows = pl.ds(pl.multiple_of(z * CHIP_NEW + here, NEW_ROWS), NEW_ROWS)
    kv_rows = pl.ds(pl.multiple_of(ALL_CACHE + x * CHIP_NEW + here, NEW_ROWS), NEW_ROWS)
    sent = []
    mine = []
    for d in (2, 1, 3, 0):
        for dc in (0, 1):
            k = d * CORES + dc
            heads = pl.ds((lax.rem(y + d, RING) * CORES + lax.rem(core + dc, CORES)) * HEADS_CORE, HEADS_CORE)
            pairs = (
                (stage.at[heads, pl.ds(1, 2)], kv.at[:, :, kv_rows]),
                (stage.at[heads, 0], q.at[:, q_rows]),
            )
            for i, (src, dst) in enumerate(pairs):
                if k:
                    copy = pltpu.make_async_remote_copy(
                        src, dst, a_send.at[i, k], a_recv.at[i, k], device_id=device(0, d, 0, dc), device_id_type=MESH
                    )
                    sent.append(copy)
                else:
                    copy = pltpu.make_async_copy(src, dst, a_recv.at[i, k])
                    mine.append(copy)
                copy.start()
    arriving = list(sent)

    angle = angles_of(cpos[...] + jnp.where(first, shot[...] * SHOT_FRAMES, 0))
    cos = jnp.cos(angle)
    sin = jnp.where(even, -jnp.sin(angle), jnp.sin(angle))
    for head in range(GROUP // HEAD_DIM):
        lanes = slice(head * HEAD_DIM, (head + 1) * HEAD_DIM)
        cstage[head, 0] = turned(ck[:, lanes], cos, sin, even)
        cstage[head, 1] = cv[:, lanes]
    c_rows = pl.ds(pl.multiple_of(x * CHIP_CACHE + core * CACHE_ROWS, CACHE_ROWS), CACHE_ROWS)
    cached = []
    for d in (2, 1, 3, 0):
        for dc in (0, 1):
            k = d * CORES + dc
            src = cstage.at[pl.ds(lax.rem(core + dc, CORES) * HEADS_CORE, HEADS_CORE)]
            dst = kv.at[:, :, c_rows]
            if k:
                copy = pltpu.make_async_remote_copy(
                    src, dst, c_send.at[k], c_recv.at[k], device_id=device(d, 0, 0, dc), device_id_type=MESH
                )
                cached.append(copy)
            else:
                copy = pltpu.make_async_copy(src, dst, c_recv.at[k])
                mine.append(copy)
            copy.start()
    sent += cached

    for copy in mine:
        copy.wait()
    for copy in arriving:
        copy.wait_recv()

    chip_kv = pl.ds(pl.multiple_of(ALL_CACHE + x * CHIP_NEW, CHIP_NEW), CHIP_NEW)
    chip_q = pl.ds(pl.multiple_of(z * CHIP_NEW, CHIP_NEW), CHIP_NEW)
    gathered = []
    for head in range(HEADS_CORE):
        of_head = []
        for d in (2, 1, 3):
            of_head.append(
                pltpu.make_async_remote_copy(
                    q.at[head, chip_q],
                    q.at[head, chip_q],
                    z_send.at[head, d],
                    z_recv.at[head, d],
                    device_id=device(0, 0, d, 0),
                    device_id_type=MESH,
                )
            )
            of_head.append(
                pltpu.make_async_remote_copy(
                    kv.at[head, :, chip_kv],
                    kv.at[head, :, chip_kv],
                    x_send.at[head, d],
                    x_recv.at[head, d],
                    device_id=device(d, 0, 0, 0),
                    device_id_type=MESH,
                )
            )
        for copy in of_head:
            copy.start()
        gathered.append(of_head)
        sent += of_head
    for copy in cached:
        copy.wait_recv()

    def o_copy(head, d, dc):
        to_z = lax.rem(z + d, RING)
        to_core = lax.rem(core + dc, CORES)
        rows = pl.ds(pl.multiple_of(to_z * CHIP_NEW + to_core * OWN, OWN), OWN)
        k = d * CORES + dc
        return pltpu.make_async_remote_copy(
            o.at[head, rows],
            ored.at[z, core, head],
            o_send.at[head, k],
            o_recv.at[head, k],
            device_id=device(0, 0, d, dc),
            device_id_type=MESH,
        )

    for head in range(HEADS_CORE):
        for copy in gathered[head]:
            copy.wait_recv()

        def attend(t, carry, head=head):
            d = lax.rem(RING + 2 - t, RING)
            to_z = lax.rem(z + d, RING)
            rows = pl.ds(pl.multiple_of(to_z * CHIP_NEW, CHIP_NEW), CHIP_NEW)
            scores = lax.dot_general(
                q[head, rows], kv[head, 0], (((1,), (1,)), ((), ())), preferred_element_type=jnp.float32
            )
            peak = jnp.max(scores, axis=1, keepdims=True)
            p = jnp.exp2((scores - peak) * SCALE2)
            total = jnp.sum(p, axis=1, keepdims=True)
            mixed = jnp.dot(p.astype(jnp.bfloat16), kv[head, 1], preferred_element_type=jnp.float32)
            o[head, rows] = (mixed / total).astype(jnp.bfloat16)
            level = peak * SCALE2 + jnp.log2(total)
            lse[rows, :] = jnp.where(lane == head, level, lse[rows, :] if head else 0.0)
            own = pl.ds(pl.multiple_of(to_z * CHIP_NEW + core * OWN, OWN), OWN)

            o_copy(head, d, 1).start()

            @pl.when(d != 0)
            def _():
                o_copy(head, d, 0).start()

            @pl.when(d == 0)
            def _():
                ored[z, core, head] = o[head, own]

            return carry

        lax.fori_loop(0, RING, attend, 0)

    stats = []
    for d in (2, 1, 3, 0):
        to_z = lax.rem(z + d, RING)
        rows = pl.ds(pl.multiple_of(to_z * CHIP_NEW, CHIP_NEW), CHIP_NEW)
        lse_t[to_z] = jnp.transpose(lse[rows, :])[0:8, :]
        for dc in (0, 1):
            k = d * CORES + dc
            if k:
                copy = pltpu.make_async_remote_copy(
                    lse_t.at[to_z],
                    lred.at[z, core],
                    l_send.at[k],
                    l_recv.at[k],
                    device_id=device(0, 0, d, dc),
                    device_id_type=MESH,
                )
                copy.start()
                stats.append(copy)
    lred[z, core] = lse_t[z]
    sent += stats

    for copy in stats:
        copy.wait_recv()
    levels = lred[...]
    share = jnp.exp2(levels - jnp.max(levels, axis=0, keepdims=True))
    share = share / jnp.sum(share, axis=0, keepdims=True)
    columns = jnp.transpose(share.reshape(RING * CORES * 8, CHIP_NEW))
    weights[:, 0 : RING * CORES * 8] = columns
    mine_w = weights[pl.ds(pl.multiple_of(core * OWN, OWN), OWN), :]
    returned = [o_copy(head, d, dc) for head in range(HEADS_CORE) for d in (2, 1, 3, 0) for dc in (0, 1) if d or dc]
    for copy in returned:
        copy.wait_recv()
    sent += returned
    attended = []
    for c in range(CORES):
        for head in range(HEADS_CORE):
            total = None
            for s in range(RING):
                at = (s * CORES + c) * 8 + head
                term = ored[s, c, head].astype(jnp.float32) * mine_w[:, at : at + 1]
                total = term if total is None else total + term
            attended.append(total.astype(jnp.bfloat16))
    attended = jnp.concatenate(attended, axis=1)

    loads[6].wait()
    summed = []
    for j in range(CHUNKS):
        cols = slice(j * CHUNK, (j + 1) * CHUNK)
        part[:, cols] = jnp.dot(attended, w[:, cols], preferred_element_type=jnp.float32).astype(jnp.bfloat16)
        of_chunk = []
        for d in (2, 1, 3):
            rows = pl.ds(pl.multiple_of(lax.rem(y + d, RING) * NEW_ROWS, NEW_ROWS), NEW_ROWS)
            copy = pltpu.make_async_remote_copy(
                part.at[rows, pl.ds(j * CHUNK, CHUNK)],
                recv.at[d, :, pl.ds(j * CHUNK, CHUNK)],
                y_send.at[j, d],
                y_recv.at[j, d],
                device_id=device(0, d, 0, 0),
                device_id_type=MESH,
            )
            copy.start()
            of_chunk.append(copy)
        summed.append(of_chunk)
        sent += of_chunk
    rows = pl.ds(pl.multiple_of(y * NEW_ROWS, NEW_ROWS), NEW_ROWS)
    for j in range(CHUNKS):
        cols = slice(j * CHUNK, (j + 1) * CHUNK)
        for copy in summed[j]:
            copy.wait_recv()
        total = part[rows, cols].astype(jnp.float32)
        for d in (1, 2, 3):
            total = total + recv[d, :, cols].astype(jnp.float32)
        out_ref[:, cols] = total.astype(jnp.bfloat16)

    for copy in sent:
        copy.wait_send()


def on_device(new_qkv, new_pos, cache_keys, cache_values, cache_pos, cache_shot, out_weight):
    bf16, f32, i32 = jnp.bfloat16, jnp.float32, jnp.int32
    dma = pltpu.SemaphoreType.DMA
    partners = RING * CORES
    return pl.pallas_call(
        kernel,
        out_shape=jax.ShapeDtypeStruct((NEW_ROWS, D), bf16),
        in_specs=[pl.BlockSpec(memory_space=pl.ANY)] * 7,
        out_specs=pl.BlockSpec(memory_space=pltpu.VMEM),
        scratch_shapes=[
            pltpu.VMEM((3, NEW_ROWS, D), bf16),
            pltpu.VMEM((3, RING * NEW_ROWS), i32),
            pltpu.VMEM((CACHE_ROWS, GROUP), bf16),
            pltpu.VMEM((CACHE_ROWS, GROUP), bf16),
            pltpu.VMEM((3, CACHE_ROWS), i32),
            pltpu.VMEM((1, CACHE_ROWS), i32),
            pltpu.VMEM((GROUP, D), bf16),
            pltpu.VMEM((RING * NEW_ROWS, HEAD_DIM), f32),
            pltpu.VMEM((D // HEAD_DIM, 3, NEW_ROWS, HEAD_DIM), bf16),
            pltpu.VMEM((GROUP // HEAD_DIM, 2, CACHE_ROWS, HEAD_DIM), bf16),
            pltpu.VMEM((HEADS_CORE, 2, KEYS, HEAD_DIM), bf16),
            pltpu.VMEM((HEADS_CORE, QUERIES, HEAD_DIM), bf16),
            pltpu.VMEM((HEADS_CORE, QUERIES, HEAD_DIM), bf16),
            pltpu.VMEM((QUERIES, HEAD_DIM), f32),
            pltpu.VMEM((RING, 8, CHIP_NEW), f32),
            pltpu.VMEM((RING, CORES, HEADS_CORE, OWN, HEAD_DIM), bf16),
            pltpu.VMEM((RING, CORES, 8, CHIP_NEW), f32),
            pltpu.VMEM((CHIP_NEW, HEAD_DIM), f32),
            pltpu.VMEM((OWN, D), bf16),
            pltpu.VMEM((RING, NEW_ROWS, D), bf16),
            dma((7,)),
            dma((2, partners)),
            dma((2, partners)),
            dma((partners,)),
            dma((partners,)),
            dma((HEADS_CORE, RING)),
            dma((HEADS_CORE, RING)),
            dma((HEADS_CORE, RING)),
            dma((HEADS_CORE, RING)),
            dma((HEADS_CORE, partners)),
            dma((HEADS_CORE, partners)),
            dma((partners,)),
            dma((partners,)),
            dma((CHUNKS, RING)),
            dma((CHUNKS, RING)),
        ],
        compiler_params=pltpu.CompilerParams(collective_id=0, has_side_effects=True, vmem_limit_bytes=63 << 20),
        name="shot_attention",
    )(
        jnp.transpose(new_qkv, (1, 0, 2)),
        new_pos,
        cache_keys,
        cache_values,
        cache_pos,
        cache_shot.reshape(1, CACHE_ROWS),
        out_weight,
    )


def solution(mesh):
    placed = (
        P(("batch", "frame", "head"), None, None),
        P("batch", "frame"),
        P(("batch", "frame"), "head"),
        P(("batch", "frame"), "head"),
        P("batch", "frame"),
        P(("batch", "frame")),
        P("head", None),
    )
    return jax.shard_map(
        on_device,
        mesh=mesh,
        in_specs=placed,
        out_specs=P(("batch", "frame", "head"), None),
        check_vma=False,
    )
```

time: 198 us -> 46.6 us (0.24)
  waiting for transfers between devices: 136 us -> 0 us
  Pallas kernels: 0 us -> 44.9 us
  matrix products: 20 us -> 0 us
  between operations: 13.4 us -> 0.01 us
  local copies, waits for them, and re-layouts: 14.6 us -> 1.54 us
  other arithmetic: 7.38 us -> 0 us
  starting transfers between devices: 5.1 us -> 0 us
    all_gather x2 -> x0, waiting for transfers between devices: 114 us -> none  [the longest x1 64.2 us: on_device(): key_rows = lax.all_gather(joined_keys, 'frame', axis=0, tiled=True)]
    pallas_call x0 -> x1, Pallas kernels: none -> 44.9 us  [on_device(): pl.pallas_call(kernel, out_shape=jax.ShapeDtypeStruct((NEW_ROWS, D), bf16...]
    dot_general x13 -> x0, matrix products: 20 us -> none  [the longest x6 9.93 us: on_device(): lax.dot_general(queries[:, lanes], key_rows[:, lanes], (((1,), (1,)), (()...]
    reduce_scatter x1 -> x0, waiting for transfers between devices: 19 us -> none  [on_device(): lax.psum_scatter(jnp.dot(attended, out_weight, preferred_element_type=jnp...]
    unnamed x21 -> x1, local copies, waits for them, and re-layouts: 12.4 us -> 1.54 us
    all_to_all x1 -> x0, starting transfers between devices: 5.01 us -> none  [on_device(): lax.all_to_all(new_qkv, 'head', split_axis=2, concat_axis=0, tiled=True)]
    all_to_all x1 -> x0, waiting for transfers between devices: 3.66 us -> none  [on_device(): lax.all_to_all(new_qkv, 'head', split_axis=2, concat_axis=0, tiled=True)]
    concatenate x2 -> x0, other arithmetic: 2.15 us -> none  [the longest x1 1.47 us: on_device(): joined_values = jnp.concatenate([cache_values, new_values], axis=0)]
  transfers between devices with their start and end apart: 4 -> 0, of which waited for: 4 -> 0; matrix products, arithmetic and copies ran while one was open for 8% -> 0% of each run, Pallas kernels for 0% -> 0%
where the time goes in v1:
time: 46.6 us; the launch traced here: 46.5 us
  Pallas kernels  44.9 us (96%)
  local copies, waits for them, and re-layouts  1.54 us (3%)
    pallas_call x1, Pallas kernels, on_device(): pl.pallas_call(kernel, out_shape=jax.ShapeDtypeStruct((NEW_ROWS, D), bf16...  44.9 us
    unnamed x1, local copies, waits for them, and re-layouts  1.54 us

profile of v1, /device:TPU:1, one launch (start us, length us, event | category | flops | bytes accessed | tf_op | source)
XLA Modules:
  0.0 46.5 jit_solution(14291742148909619544)
XLA Ops:
  0.0 44.9 %shot_attention.1 = bf16[16,3072]{1,0:T(8,128)(2,1)} custom-call(bf16[3,16,3072]{2,1,0:T(8,128)(2,1)} %bitcast.2, s32[3,64]{1,0:T(4,128)} %npos_hbm.1, bf16[32,768]{1,0:T(8,128)(2,1)} %ck_hbm.1, bf16[32,768]{1,0:T(8,128)(2,1)} %cv_hbm.1, s32[3,32]{1,0:T(4,128)} %cpos_hbm.1, s32[1,32]{1,0:T(1,128)} %bitcast.3, bf16[768,3072]{1,0:T(8,128)(2,1)} %w_hbm.1), custom_call_target="tpu_custom_call" | custom-call | tf_op jit(solution)/shard_map/shot_attention/pallas_call | solution.py:388
  44.9 1.5 %copy.9 = bf16[16,3072]{1,0:T(8,128)(2,1)} copy(bf16[16,3072]{1,0:T(8,128)(2,1)} %shot_attention.1) | data formatting | bytes 196608

commit v2 on v1

--- a/solution.py
+++ b/solution.py
@@ -88,6 +88,9 @@
     part,
     recv,
     in_sem,
+    heard,
+    f_send,
+    f_recv,
     a_send,
     a_recv,
     c_send,
@@ -114,7 +117,14 @@
         to = (lax.rem(z + dz, RING) * RING + lax.rem(x + dx, RING)) * CORES + lax.rem(core + dc, CORES)
         return (to, lax.rem(y + dy, RING), batch)
 
+    def partners():
+        for to_core in (0, 1):
+            for d in (2, 1, 3):
+                yield d, lax.rem(core + to_core, CORES)
+        yield 0, 1
+
     barrier = pltpu.get_barrier_semaphore()
+    crossed = [(0, dy, dz, c) for dz in (2, 1, 3, 0) for c in (0, 1) for dy in (2, 1, 3, 0) if dy or dz or c]
     greeted = [(0, 0, 0, 1)]
     for d in (2, 1, 3):
         for dc in (0, 1):
@@ -165,33 +175,6 @@
         return carry
 
     lax.fori_loop(0, D // (HEAD_DIM * HEADS_CORE), rotate_new, 0)
-    pl.semaphore_wait(barrier, len(greeted))
-
-    here = pl.multiple_of(core * OWN + y * NEW_ROWS, NEW_ROWS)
-    q_rows = pl.ds(pl.multiple_of(z * CHIP_NEW + here, NEW_ROWS), NEW_ROWS)
-    kv_rows = pl.ds(pl.multiple_of(ALL_CACHE + x * CHIP_NEW + here, NEW_ROWS), NEW_ROWS)
-    sent = []
-    mine = []
-    for d in (2, 1, 3, 0):
-        for dc in (0, 1):
-            k = d * CORES + dc
-            heads = pl.ds((lax.rem(y + d, RING) * CORES + lax.rem(core + dc, CORES)) * HEADS_CORE, HEADS_CORE)
-            pairs = (
-                (stage.at[heads, pl.ds(1, 2)], kv.at[:, :, kv_rows]),
-                (stage.at[heads, 0], q.at[:, q_rows]),
-            )
-            for i, (src, dst) in enumerate(pairs):
-                if k:
-                    copy = pltpu.make_async_remote_copy(
-                        src, dst, a_send.at[i, k], a_recv.at[i, k], device_id=device(0, d, 0, dc), device_id_type=MESH
-                    )
-                    sent.append(copy)
-                else:
-                    copy = pltpu.make_async_copy(src, dst, a_recv.at[i, k])
-                    mine.append(copy)
-                copy.start()
-    arriving = list(sent)
-
     angle = angles_of(cpos[...] + jnp.where(first, shot[...] * SHOT_FRAMES, 0))
     cos = jnp.cos(angle)
     sin = jnp.where(even, -jnp.sin(angle), jnp.sin(angle))
@@ -199,61 +182,122 @@
         lanes = slice(head * HEAD_DIM, (head + 1) * HEAD_DIM)
         cstage[head, 0] = turned(ck[:, lanes], cos, sin, even)
         cstage[head, 1] = cv[:, lanes]
+    pl.semaphore_wait(barrier, len(greeted))
+    for d in (2, 1, 3):
+        pl.semaphore_signal(heard, inc=1, device_id=device(0, d, 0, 0), device_id_type=MESH)
+
+    here = pl.multiple_of(core * OWN + y * NEW_ROWS, NEW_ROWS)
+    q_rows = pl.ds(pl.multiple_of(z * CHIP_NEW + here, NEW_ROWS), NEW_ROWS)
+    kv_rows = pl.ds(pl.multiple_of(ALL_CACHE + x * CHIP_NEW + here, NEW_ROWS), NEW_ROWS)
+    sent = []
+
+    def scatter(sems, offsets, parts):
+        copies = []
+        for d, dc in partners():
+            k = d * CORES + dc
+            src, dst, to = parts(d, dc)
+            copy = pltpu.make_async_remote_copy(
+                src, dst, sems[0].at[offsets, k], sems[1].at[offsets, k], device_id=to, device_id_type=MESH
+            )
+            sent.append(copy)
+            copy.start()
+            copies.append(copy)
+        src, dst, _ = parts(0, 0)
+        copy = pltpu.make_async_copy(src, dst, sems[1].at[offsets, 0])
+        copy.start()
+        copies.append(copy)
+        return copies
+
+    def arrive(copies):
+        for copy in copies[:-1]:
+            copy.wait_recv()
+        copies[-1].wait()
+
+    def new_part(first, heads, of_q):
+        def parts(d, dc):
+            to = (lax.rem(y + d, RING) * CORES + lax.rem(core + dc, CORES)) * HEADS_CORE
+            src = stage.at[pl.ds(to + first, heads)]
+            own = pl.ds(first, heads)
+            if of_q:
+                return src.at[:, 0], q.at[own, q_rows], device(0, d, 0, dc)
+            return src.at[:, pl.ds(1, 2)], kv.at[own, :, kv_rows], device(0, d, 0, dc)
+
+        return parts
+
+    def cache_part(d, dc):
+        src = cstage.at[pl.ds(lax.rem(core + dc, CORES) * HEADS_CORE, HEADS_CORE)]
+        return src, kv.at[:, :, c_rows], device(d, 0, 0, dc)
+
     c_rows = pl.ds(pl.multiple_of(x * CHIP_CACHE + core * CACHE_ROWS, CACHE_ROWS), CACHE_ROWS)
-    cached = []
-    for d in (2, 1, 3, 0):
-        for dc in (0, 1):
-            k = d * CORES + dc
-            src = cstage.at[pl.ds(lax.rem(core + dc, CORES) * HEADS_CORE, HEADS_CORE)]
-            dst = kv.at[:, :, c_rows]
-            if k:
-                copy = pltpu.make_async_remote_copy(
-                    src, dst, c_send.at[k], c_recv.at[k], device_id=device(d, 0, 0, dc), device_id_type=MESH
-                )
-                cached.append(copy)
-            else:
-                copy = pltpu.make_async_copy(src, dst, c_recv.at[k])
-                mine.append(copy)
-            copy.start()
-    sent += cached
-
-    for copy in mine:
-        copy.wait()
-    for copy in arriving:
-        copy.wait_recv()
-
     chip_kv = pl.ds(pl.multiple_of(ALL_CACHE + x * CHIP_NEW, CHIP_NEW), CHIP_NEW)
     chip_q = pl.ds(pl.multiple_of(z * CHIP_NEW, CHIP_NEW), CHIP_NEW)
-    gathered = []
-    for head in range(HEADS_CORE):
-        of_head = []
-        for d in (2, 1, 3):
-            of_head.append(
-                pltpu.make_async_remote_copy(
-                    q.at[head, chip_q],
-                    q.at[head, chip_q],
-                    z_send.at[head, d],
-                    z_recv.at[head, d],
-                    device_id=device(0, 0, d, 0),
-                    device_id_type=MESH,
-                )
+
+    def along_x(head):
+        copies = [
+            pltpu.make_async_remote_copy(
+                kv.at[head, :, chip_kv],
+                kv.at[head, :, chip_kv],
+                x_send.at[head, d],
+                x_recv.at[head, d],
+                device_id=device(d, 0, 0, 0),
+                device_id_type=MESH,
             )
-            of_head.append(
-                pltpu.make_async_remote_copy(
-                    kv.at[head, :, chip_kv],
-                    kv.at[head, :, chip_kv],
-                    x_send.at[head, d],
-                    x_recv.at[head, d],
-                    device_id=device(d, 0, 0, 0),
-                    device_id_type=MESH,
-                )
+            for d in (2, 1, 3)
+        ]
+        for copy in copies:
+            copy.start()
+        sent.extend(copies)
+        return copies
+
+    def along_z(head):
+        copies = [
+            pltpu.make_async_remote_copy(
+                q.at[head, chip_q],
+                q.at[head, chip_q],
+                z_send.at[head, d],
+                z_recv.at[head, d],
+                device_id=device(0, 0, d, 0),
+                device_id_type=MESH,
             )
-        for copy in of_head:
+            for d in (2, 1, 3)
+        ]
+        for copy in copies:
             copy.start()
-        gathered.append(of_head)
-        sent += of_head
-    for copy in cached:
-        copy.wait_recv()
+        sent.extend(copies)
+        return copies
+
+    a_sems = (a_send, a_recv)
+    kv_in = [scatter(a_sems, 1, new_part(0, 1, False))]
+    cached = scatter((c_send, c_recv), 0, cache_part)
+    q_in = scatter(a_sems, 0, new_part(1, 2, True))
+    kv_in.append(scatter(a_sems, 2, new_part(1, 2, False)))
+    pl.semaphore_wait(heard, 3)
+    straight = []
+    for dx, dy, dz, at_core in crossed:
+        dc = lax.rem(core + at_core, CORES) if dy or dz else 1
+        to = (lax.rem(y + dy, RING) * CORES + lax.rem(core + dc, CORES)) * HEADS_CORE
+        copy = pltpu.make_async_remote_copy(
+            stage.at[to, 0],
+            q.at[0, q_rows],
+            f_send.at[0],
+            f_recv.at[0],
+            device_id=device(dx, dy, dz, dc),
+            device_id_type=MESH,
+        )
+        copy.start()
+    own_q = pltpu.make_async_copy(stage.at[(y * CORES + core) * HEADS_CORE, 0], q.at[0, q_rows], f_recv.at[1])
+    own_q.start()
+
+    arrive(kv_in[0])
+    gathered_x = [along_x(0)]
+    arrive(q_in)
+    gathered_z = [[], along_z(1), along_z(2)]
+    arrive(kv_in[1])
+    gathered_x += [along_x(1), along_x(2)]
+    arrive(cached)
+    whole = q.at[0, pl.ds(0, QUERIES - NEW_ROWS)]
+    pltpu.make_async_copy(whole, whole, f_recv.at[0]).wait()
+    own_q.wait()
 
     def o_copy(head, d, dc):
         to_z = lax.rem(z + d, RING)
@@ -270,49 +314,22 @@
         )
 
     for head in range(HEADS_CORE):
-        for copy in gathered[head]:
+        for copy in gathered_x[head] + gathered_z[head]:
             copy.wait_recv()
-
-        def attend(t, carry, head=head):
-            d = lax.rem(RING + 2 - t, RING)
-            to_z = lax.rem(z + d, RING)
-            rows = pl.ds(pl.multiple_of(to_z * CHIP_NEW, CHIP_NEW), CHIP_NEW)
-            scores = lax.dot_general(
-                q[head, rows], kv[head, 0], (((1,), (1,)), ((), ())), preferred_element_type=jnp.float32
-            )
-            peak = jnp.max(scores, axis=1, keepdims=True)
-            p = jnp.exp2((scores - peak) * SCALE2)
-            total = jnp.sum(p, axis=1, keepdims=True)
-            mixed = jnp.dot(p.astype(jnp.bfloat16), kv[head, 1], preferred_element_type=jnp.float32)
-            o[head, rows] = (mixed / total).astype(jnp.bfloat16)
-            level = peak * SCALE2 + jnp.log2(total)
-            lse[rows, :] = jnp.where(lane == head, level, lse[rows, :] if head else 0.0)
-            own = pl.ds(pl.multiple_of(to_z * CHIP_NEW + core * OWN, OWN), OWN)
-
-            o_copy(head, d, 1).start()
-
-            @pl.when(d != 0)
-            def _():
-                o_copy(head, d, 0).start()
-
-            @pl.when(d == 0)
-            def _():
-                ored[z, core, head] = o[head, own]
-
-            return carry
-
-        lax.fori_loop(0, RING, attend, 0)
-
-    stats = []
-    for d in (2, 1, 3, 0):
-        to_z = lax.rem(z + d, RING)
-        rows = pl.ds(pl.multiple_of(to_z * CHIP_NEW, CHIP_NEW), CHIP_NEW)
-        lse_t[to_z] = jnp.transpose(lse[rows, :])[0:8, :]
-        for dc in (0, 1):
-            k = d * CORES + dc
-            if k:
+        scores = lax.dot_general(q[head], kv[head, 0], (((1,), (1,)), ((), ())), preferred_element_type=jnp.float32)
+        peak = jnp.max(scores, axis=1, keepdims=True)
+        p = jnp.exp2((scores - peak) * SCALE2)
+        total = jnp.sum(p, axis=1, keepdims=True)
+        level = peak * SCALE2 + jnp.log2(total)
+        lse[...] = jnp.where(lane == head, level, lse[...] if head else 0.0)
+        if head == HEADS_CORE - 1:
+            stats = []
+            for s in range(RING):
+                lse_t[s] = jnp.transpose(lse[s * CHIP_NEW : (s + 1) * CHIP_NEW, :])[0:8, :]
+            for d, dc in partners():
+                k = d * CORES + dc
                 copy = pltpu.make_async_remote_copy(
-                    lse_t.at[to_z],
+                    lse_t.at[lax.rem(z + d, RING)],
                     lred.at[z, core],
                     l_send.at[k],
                     l_recv.at[k],
@@ -321,8 +338,14 @@
                 )
                 copy.start()
                 stats.append(copy)
-    lred[z, core] = lse_t[z]
-    sent += stats
+            lred[z, core] = lse_t[z]
+            sent += stats
+        mixed = jnp.dot(p.astype(jnp.bfloat16), kv[head, 1], preferred_element_type=jnp.float32)
+        o[head] = (mixed / total).astype(jnp.bfloat16)
+        for d, dc in partners():
+            o_copy(head, d, dc).start()
+        own = pl.ds(pl.multiple_of(z * CHIP_NEW + core * OWN, OWN), OWN)
+        ored[z, core, head] = o[head, own]
 
     for copy in stats:
         copy.wait_recv()
@@ -332,7 +355,7 @@
     columns = jnp.transpose(share.reshape(RING * CORES * 8, CHIP_NEW))
     weights[:, 0 : RING * CORES * 8] = columns
     mine_w = weights[pl.ds(pl.multiple_of(core * OWN, OWN), OWN), :]
-    returned = [o_copy(head, d, dc) for head in range(HEADS_CORE) for d in (2, 1, 3, 0) for dc in (0, 1) if d or dc]
+    returned = [o_copy(head, d, dc) for head in range(HEADS_CORE) for d, dc in partners()]
     for copy in returned:
         copy.wait_recv()
     sent += returned
@@ -379,6 +402,7 @@
 
     for copy in sent:
         copy.wait_send()
+    pltpu.make_async_copy(whole, whole, f_send.at[0]).wait()
 
 
 def on_device(new_qkv, new_pos, cache_keys, cache_values, cache_pos, cache_shot, out_weight):
@@ -412,10 +436,13 @@
             pltpu.VMEM((OWN, D), bf16),
             pltpu.VMEM((RING, NEW_ROWS, D), bf16),
             dma((7,)),
-            dma((2, partners)),
-            dma((2, partners)),
-            dma((partners,)),
-            dma((partners,)),
+            pltpu.SemaphoreType.REGULAR,
+            dma((1,)),
+            dma((2,)),
+            dma((4, partners)),
+            dma((4, partners)),
+            dma((1, partners)),
+            dma((1, partners)),
             dma((HEADS_CORE, RING)),
             dma((HEADS_CORE, RING)),
             dma((HEADS_CORE, RING)),
@@ -427,16 +454,21 @@
             dma((CHUNKS, RING)),
             dma((CHUNKS, RING)),
         ],
-        compiler_params=pltpu.CompilerParams(collective_id=0, has_side_effects=True, vmem_limit_bytes=63 << 20),
+        compiler_params=pltpu.CompilerParams(collective_id=0, has_side_effects=True, vmem_limit_bytes=32 << 20),
         name="shot_attention",
     )(
-        jnp.transpose(new_qkv, (1, 0, 2)),
-        new_pos,
-        cache_keys,
-        cache_values,
-        cache_pos,
-        cache_shot.reshape(1, CACHE_ROWS),
-        out_weight,
+        *(
+            pltpu.with_memory_space_constraint(a, pltpu.HBM)
+            for a in (
+                jnp.transpose(new_qkv, (1, 0, 2)),
+                new_pos,
+                cache_keys,
+                cache_values,
+                cache_pos,
+                cache_shot.reshape(1, CACHE_ROWS),
+                out_weight,
+            )
+        )
     )
 
 

time: 46.6 us -> 43.4 us (0.931)
  Pallas kernels: 44.9 us -> 42.6 us
  local copies, waits for them, and re-layouts: 1.54 us -> 0.64 us
    pallas_call x1, Pallas kernels: 44.9 us -> 42.6 us  [on_device(): pl.pallas_call(kernel, out_shape=jax.ShapeDtypeStruct((NEW_ROWS, D), bf16...]
    unnamed x1, local copies, waits for them, and re-layouts: 1.54 us -> 0.64 us
where the time goes in v2:
time: 43.4 us; the launch traced here: 43.3 us
  Pallas kernels  42.6 us (98%)
  local copies, waits for them, and re-layouts  0.64 us (1%)
    pallas_call x1, Pallas kernels, on_device(): pl.pallas_call(kernel, out_shape=jax.ShapeDtypeStruct((NEW_ROWS, D), bf16...  42.6 us

profile of v2, /device:TPU:1, one launch (start us, length us, event | category | flops | bytes accessed | tf_op | source)
XLA Modules:
  0.0 43.3 jit_solution(8276125821053061685)
XLA Ops:
  0.0 42.6 %shot_attention.1 = bf16[16,3072]{1,0:T(8,128)(2,1)S(1)} custom-call(bf16[3,16,3072]{2,1,0:T(8,128)(2,1)} %bitcast.2, s32[3,64]{1,0:T(4,128)} %npos_hbm.1, bf16[32,768]{1,0:T(8,128)(2,1)} %ck_hbm.1, bf16[32,768]{1,0:T(8,128)(2,1)} %cv_hbm.1, s32[3,32]{1,0:T(4,128)} %cpos_hbm.1, s32[1,32]{1,0:T(1,128)} %bitcast.3, bf16[768,3072]{1,0:T(8,128)(2,1)} %w_hbm.1), custom_call_target="tpu_custom_call" | custom-call | tf_op jit(solution)/shard_map/shot_attention/pallas_call | solution.py:412
  42.6 0.6 %copy.9 = bf16[16,3072]{1,0:T(8,128)(2,1)} copy(bf16[16,3072]{1,0:T(8,128)(2,1)S(1)} %shot_attention.1) | data formatting | bytes 196608

commit v3 on v2

--- a/solution.py
+++ b/solution.py
@@ -89,6 +89,7 @@
     recv,
     in_sem,
     heard,
+    told,
     f_send,
     f_recv,
     a_send,
@@ -124,14 +125,14 @@
         yield 0, 1
 
     barrier = pltpu.get_barrier_semaphore()
+    for d in (2, 1, 3):
+        pl.semaphore_signal(barrier, inc=1, device_id=device(0, 0, d, core), device_id_type=MESH)
+    for d in (2, 1, 3):
+        pl.semaphore_signal(barrier, inc=1, device_id=device(0, d, 0, 1 - core), device_id_type=MESH)
+        pl.semaphore_signal(barrier, inc=1, device_id=device(d, 0, 0, 1 - core), device_id_type=MESH)
+    pl.semaphore_signal(barrier, inc=1, device_id=device(0, 0, 0, 1), device_id_type=MESH)
+
     crossed = [(0, dy, dz, c) for dz in (2, 1, 3, 0) for c in (0, 1) for dy in (2, 1, 3, 0) if dy or dz or c]
-    greeted = [(0, 0, 0, 1)]
-    for d in (2, 1, 3):
-        for dc in (0, 1):
-            greeted += [(0, 0, d, dc), (d, 0, 0, dc), (0, d, 0, dc)]
-    for g in greeted:
-        pl.semaphore_signal(barrier, inc=1, device_id=device(*g), device_id_type=MESH)
-
     loads = [
         pltpu.make_async_copy(a, b, in_sem.at[i])
         for i, (a, b) in enumerate(
@@ -182,9 +183,14 @@
         lanes = slice(head * HEAD_DIM, (head + 1) * HEAD_DIM)
         cstage[head, 0] = turned(ck[:, lanes], cos, sin, even)
         cstage[head, 1] = cv[:, lanes]
-    pl.semaphore_wait(barrier, len(greeted))
-    for d in (2, 1, 3):
-        pl.semaphore_signal(heard, inc=1, device_id=device(0, d, 0, 0), device_id_type=MESH)
+    @pl.when(core == 1)
+    def _():
+        pl.semaphore_wait(barrier, 2 * CORES * (RING - 1) + 1)
+        pl.semaphore_signal(heard, inc=1, device_id=device(0, 0, 0, 1), device_id_type=MESH)
+
+    @pl.when(core == 0)
+    def _():
+        pl.semaphore_wait(heard, 1)
 
     here = pl.multiple_of(core * OWN + y * NEW_ROWS, NEW_ROWS)
     q_rows = pl.ds(pl.multiple_of(z * CHIP_NEW + here, NEW_ROWS), NEW_ROWS)
@@ -266,12 +272,28 @@
         sent.extend(copies)
         return copies
 
+    def flush(copies):
+        for copy in copies:
+            copy.wait_send()
+            sent[:] = [s for s in sent if s is not copy]
+
     a_sems = (a_send, a_recv)
     kv_in = [scatter(a_sems, 1, new_part(0, 1, False))]
+    q_in = scatter(a_sems, 0, new_part(1, 2, True))
     cached = scatter((c_send, c_recv), 0, cache_part)
-    q_in = scatter(a_sems, 0, new_part(1, 2, True))
     kv_in.append(scatter(a_sems, 2, new_part(1, 2, False)))
-    pl.semaphore_wait(heard, 3)
+    @pl.when(core == 0)
+    def _():
+        pl.semaphore_wait(barrier, CORES * (RING - 1) + 1)
+        pl.semaphore_signal(heard, inc=1, device_id=device(0, 0, 0, 1), device_id_type=MESH)
+
+    @pl.when(core == 1)
+    def _():
+        pl.semaphore_wait(heard, 1)
+
+    for d in (2, 1, 3):
+        pl.semaphore_signal(told, inc=1, device_id=device(0, d, 0, 0), device_id_type=MESH)
+    pl.semaphore_wait(told, 3)
     straight = []
     for dx, dy, dz, at_core in crossed:
         dc = lax.rem(core + at_core, CORES) if dy or dz else 1
@@ -291,9 +313,11 @@
     arrive(kv_in[0])
     gathered_x = [along_x(0)]
     arrive(q_in)
-    gathered_z = [[], along_z(1), along_z(2)]
+    gathered_z = [[], along_z(1)]
+    gathered_z.append(along_z(2))
     arrive(kv_in[1])
-    gathered_x += [along_x(1), along_x(2)]
+    gathered_x.append(along_x(1))
+    gathered_x.append(along_x(2))
     arrive(cached)
     whole = q.at[0, pl.ds(0, QUERIES - NEW_ROWS)]
     pltpu.make_async_copy(whole, whole, f_recv.at[0]).wait()
@@ -436,6 +460,7 @@
             pltpu.VMEM((OWN, D), bf16),
             pltpu.VMEM((RING, NEW_ROWS, D), bf16),
             dma((7,)),
+            pltpu.SemaphoreType.REGULAR,
             pltpu.SemaphoreType.REGULAR,
             dma((1,)),
             dma((2,)),

time: 43.4 us -> 42.5 us (0.979)
  Pallas kernels: 42.6 us -> 41.7 us
    pallas_call x1, Pallas kernels: 42.6 us -> 41.7 us  [on_device(): pl.pallas_call(kernel, out_shape=jax.ShapeDtypeStruct((NEW_ROWS, D), bf16...]
where the time goes in v3:
time: 42.5 us; the launch traced here: 42.4 us
  Pallas kernels  41.7 us (98%)
  local copies, waits for them, and re-layouts  0.64 us (2%)
    pallas_call x1, Pallas kernels, on_device(): pl.pallas_call(kernel, out_shape=jax.ShapeDtypeStruct((NEW_ROWS, D), bf16...  41.7 us

profile of v3, /device:TPU:1, one launch (start us, length us, event | category | flops | bytes accessed | tf_op | source)
XLA Modules:
  0.0 42.4 jit_solution(369584787016040625)
XLA Ops:
  0.0 41.7 %shot_attention.1 = bf16[16,3072]{1,0:T(8,128)(2,1)S(1)} custom-call(bf16[3,16,3072]{2,1,0:T(8,128)(2,1)} %bitcast.2, s32[3,64]{1,0:T(4,128)} %npos_hbm.1, bf16[32,768]{1,0:T(8,128)(2,1)} %ck_hbm.1, bf16[32,768]{1,0:T(8,128)(2,1)} %cv_hbm.1, s32[3,32]{1,0:T(4,128)} %cpos_hbm.1, s32[1,32]{1,0:T(1,128)} %bitcast.3, bf16[768,3072]{1,0:T(8,128)(2,1)} %w_hbm.1), custom_call_target="tpu_custom_call" | custom-call | tf_op jit(solution)/shard_map/shot_attention/pallas_call | solution.py:436
  41.8 0.6 %copy.9 = bf16[16,3072]{1,0:T(8,128)(2,1)} copy(bf16[16,3072]{1,0:T(8,128)(2,1)S(1)} %shot_attention.1) | data formatting | bytes 196608

commit v4 on v3

--- a/solution.py
+++ b/solution.py
@@ -25,7 +25,7 @@
 OWN = RING * NEW_ROWS
 D = 3072
 GROUP = D // RING
-CHUNKS = 4
+CHUNKS = 3
 CHUNK = D // CHUNKS
 SCALE2 = math.log2(math.e) / math.sqrt(HEAD_DIM)
 MESH = pl.DeviceIdType.MESH
@@ -379,19 +379,19 @@
     columns = jnp.transpose(share.reshape(RING * CORES * 8, CHIP_NEW))
     weights[:, 0 : RING * CORES * 8] = columns
     mine_w = weights[pl.ds(pl.multiple_of(core * OWN, OWN), OWN), :]
-    returned = [o_copy(head, d, dc) for head in range(HEADS_CORE) for d, dc in partners()]
-    for copy in returned:
-        copy.wait_recv()
-    sent += returned
-    attended = []
-    for c in range(CORES):
-        for head in range(HEADS_CORE):
+    attended = [None] * (CORES * HEADS_CORE)
+    for head in range(HEADS_CORE):
+        returned = [o_copy(head, d, dc) for d, dc in partners()]
+        for copy in returned:
+            copy.wait_recv()
+        sent += returned
+        for c in range(CORES):
             total = None
             for s in range(RING):
                 at = (s * CORES + c) * 8 + head
                 term = ored[s, c, head].astype(jnp.float32) * mine_w[:, at : at + 1]
                 total = term if total is None else total + term
-            attended.append(total.astype(jnp.bfloat16))
+            attended[c * HEADS_CORE + head] = total.astype(jnp.bfloat16)
     attended = jnp.concatenate(attended, axis=1)
 
     loads[6].wait()

time: 42.5 us -> 42.3 us (level)
  no operation moved by 1% of the time
where the time goes in v4:
time: 42.3 us; the launch traced here: 42.2 us
  Pallas kernels  41.5 us (98%)
  local copies, waits for them, and re-layouts  0.64 us (2%)
    pallas_call x1, Pallas kernels, on_device(): pl.pallas_call(kernel, out_shape=jax.ShapeDtypeStruct((NEW_ROWS, D), bf16...  41.5 us

profile of v4, /device:TPU:1, one launch (start us, length us, event | category | flops | bytes accessed | tf_op | source)
XLA Modules:
  0.0 42.2 jit_solution(5562968171491590498)
XLA Ops:
  0.0 41.5 %shot_attention.1 = bf16[16,3072]{1,0:T(8,128)(2,1)S(1)} custom-call(bf16[3,16,3072]{2,1,0:T(8,128)(2,1)} %bitcast.2, s32[3,64]{1,0:T(4,128)} %npos_hbm.1, bf16[32,768]{1,0:T(8,128)(2,1)} %ck_hbm.1, bf16[32,768]{1,0:T(8,128)(2,1)} %cv_hbm.1, s32[3,32]{1,0:T(4,128)} %cpos_hbm.1, s32[1,32]{1,0:T(1,128)} %bitcast.3, bf16[768,3072]{1,0:T(8,128)(2,1)} %w_hbm.1), custom_call_target="tpu_custom_call" | custom-call | tf_op jit(solution)/shard_map/shot_attention/pallas_call | solution.py:436
  41.5 0.6 %copy.9 = bf16[16,3072]{1,0:T(8,128)(2,1)} copy(bf16[16,3072]{1,0:T(8,128)(2,1)S(1)} %shot_attention.1) | data formatting | bytes 196608
